TPU v7x, 32 devices: a whole 2x2x4 slice. The times are simulated.
32 devices in a mesh: groups: 2 (over x), dom: 8 (over z, y), slab: 2 (over core).
Axes of the slice: x: 2, y: 2, z: 4, core: 2. Of those that a mesh axis runs over, the one named last changes fastest.
Arguments:
- features: bfloat16 [2, 2048, 512], P('slab', ('groups', 'dom')), parts along dimension 1, may hold values from -6 to 6
- orbitals: int32 [2, 2048], P('slab', ('groups', 'dom')), parts along dimension 1, may hold values from 4 to 13
- pair_list: int32 [2, 32768, 2], P('slab', ('groups', 'dom')), parts along dimension 1, may hold values from 0 to 671, as said below
- owners: int32 [2, 32768, 1], P('slab', ('groups', 'dom')), parts along dimension 1, may hold values from 0 to 7; in each aligned block of 2048 rows (0 to 2047, 2048 to 4095, ..., all dimensions but the last counted through in order) at most 384 rows name the same one
- edge_feats: bfloat16 [2, 32768, 128], P('slab', ('groups', 'dom')), parts along dimension 1, may hold values from -6 to 6
- cotangent: bfloat16 [2, 49152, 169], P('slab', ('groups', 'dom')), parts along dimension 1, may hold values from -6 to 6
- w_pair: bfloat16 [512, 512], replicated, may hold values from -0.25 to 0.25
- w_edge: bfloat16 [128, 512], replicated, may hold values from -0.5 to 0.5
- w_block: bfloat16 [512, 169], replicated, may hold values from -0.25 to 0.25
Outputs:
- block_out: bfloat16 [2, 49152, 169], P('slab', ('groups', 'dom')), parts along dimension 1
- atom_grads: float32 [2, 2048, 512], P('slab', ('groups', 'dom')), parts along dimension 1
- grad_pair: float32 [1024, 512], P('groups'), parts along dimension 0
- grad_edge: float32 [256, 512], P('groups'), parts along dimension 0
- grad_block: float32 [1024, 169], P('groups'), parts along dimension 0
There are 2 independent parts, one for each index of `groups`. A program takes and returns all parts, laid end to end along the dimension named above; an argument that names none is the same for every part. Nothing has to cross between parts.
Inputs may be any that keep to these rules, and one draw needn't show every extreme that they name: pair_list[s, q, 0] lies in 0 to 127 and is 0 for the first task of each domain. With r = pair_list[s, q, 1] % 384: r lies in 96 to 287, and pair_list[s, q, 1] is below 768; the first task of each domain has the largest such value. `owners`: among the 2048 tasks of one domain, at most 384 have the same owner.
All inputs are finite; a program needn't handle non-finite values.
Results may differ from a plain program's by a relative error of at most 0.0056.
Values may be sent and summed in bfloat16 or wider, within the bound.
A program may use at most 64 MiB of HBM per device.

v0:
```python
import jax
import jax.numpy as jnp
from jax import lax
from jax.sharding import PartitionSpec as P

ORB = 13


def padded(cells, sides, width):
    for axis, dim in sides:
        count = lax.axis_size(axis)
        head = lax.slice_in_dim(cells, 0, width, axis=dim)
        tail = lax.slice_in_dim(cells, cells.shape[dim] - width, cells.shape[dim], axis=dim)
        cells = jnp.concatenate(
            [
                lax.ppermute(tail, axis, [(i, (i + 1) % count) for i in range(count)]),
                cells,
                lax.ppermute(head, axis, [((i + 1) % count, i) for i in range(count)]),
            ],
            axis=dim,
        )
    return cells


def from_partner(x, axis, apart):
    return lax.ppermute(x, axis, [(i, i ^ 1 << apart) for i in range(lax.axis_size(axis))])


def shifted(x, axis, by):
    devices = lax.axis_size(axis)
    return lax.ppermute(x, axis, [(i, (i + by) % devices) for i in range(devices)])


def shards(features, orbitals, pair_list, owners, edge_feats, cotangent, w_pair, w_edge, w_block):
    atoms = features[0]
    count_atoms = atoms.shape[0]
    domains = lax.axis_size("dom")
    capacity = cotangent.shape[1] // domains
    block_size = w_block.shape[1]
    own_idx = pair_list[0, :, 0]
    near_raw = pair_list[0, :, 1]
    counts_wire = orbitals.astype(jnp.bfloat16)
    rest = near_raw % (3 * count_atoms)
    ext_feat, ext_count = (
        padded(features, (("dom", 1),), count_atoms),
        padded(counts_wire, (("dom", 1),), count_atoms),
    )
    far_feat, far_count = from_partner((ext_feat, ext_count), "slab", 0)
    span = count_atoms + 2 * count_atoms
    near_idx = jnp.where(near_raw >= 3 * count_atoms, span, 0) + rest - count_atoms + count_atoms
    table_feat = jnp.concatenate([ext_feat[0], far_feat[0]], axis=0)
    table_count = jnp.concatenate([ext_count[0], far_count[0]], axis=0)
    own_hits = own_idx[:, None] == jnp.arange(count_atoms, dtype=jnp.int32)[None, :]
    near_hits = near_idx[:, None] == jnp.arange(2 * span, dtype=jnp.int32)[None, :]
    x_own = jnp.dot(
        own_hits.astype(jnp.bfloat16), atoms, preferred_element_type=jnp.float32
    ).astype(jnp.bfloat16)
    x_near = jnp.dot(
        near_hits.astype(jnp.bfloat16), table_feat, preferred_element_type=jnp.float32
    ).astype(jnp.bfloat16)
    n_own = orbitals[0][own_idx]
    n_near = table_count[near_idx].astype(jnp.int32)
    prod = (x_own.astype(jnp.float32) * x_near.astype(jnp.float32)).astype(jnp.bfloat16)
    edges = edge_feats[0]
    pre = jnp.dot(prod, w_pair, preferred_element_type=jnp.float32) + jnp.dot(
        edges, w_edge, preferred_element_type=jnp.float32
    )
    act = jax.nn.silu(pre).astype(jnp.bfloat16)
    entry = jnp.arange(block_size, dtype=jnp.int32)
    mask = ((entry // ORB)[None, :] < n_own[:, None]) & ((entry % ORB)[None, :] < n_near[:, None])
    raw = jnp.dot(act, w_block, preferred_element_type=jnp.float32)
    blocks = jnp.where(mask, raw, 0.0).astype(jnp.bfloat16)
    owner = owners[0, :, 0]
    onehot = (owner[:, None] == jnp.arange(domains, dtype=jnp.int32)[None, :]).astype(jnp.int32)
    rank = jnp.cumsum(onehot, axis=0)
    slot = jnp.sum(onehot * rank, axis=1) - 1
    target = owner * capacity + slot
    outgoing = jnp.zeros((domains * capacity, block_size), jnp.bfloat16).at[target].set(blocks)
    received = lax.all_to_all(outgoing, "dom", split_axis=0, concat_axis=0, tiled=True)
    returned = lax.all_to_all(cotangent[0], "dom", split_axis=0, concat_axis=0, tiled=True)
    cot = returned[target]
    dblock = jnp.where(mask, cot, jnp.zeros_like(cot))
    dact = jnp.dot(dblock, w_block.T, preferred_element_type=jnp.float32)
    sigm = jax.nn.sigmoid(pre)
    dpre = (dact * sigm * (1.0 + pre * (1.0 - sigm))).astype(jnp.bfloat16)
    dprod = jnp.dot(dpre, w_pair.T, preferred_element_type=jnp.float32)
    grad_own = jnp.dot(
        own_hits.astype(jnp.float32).T,
        dprod * x_near.astype(jnp.float32),
        precision=lax.Precision.HIGHEST,
        preferred_element_type=jnp.float32,
    )
    grad_table = jnp.dot(
        near_hits.astype(jnp.float32).T,
        dprod * x_own.astype(jnp.float32),
        precision=lax.Precision.HIGHEST,
        preferred_element_type=jnp.float32,
    )
    from_other = from_partner(grad_table[span:].astype(jnp.bfloat16), "slab", 0).astype(jnp.float32)
    ext_grad = grad_table[:span] + from_other
    from_next = shifted(ext_grad[:count_atoms].astype(jnp.bfloat16), "dom", -1).astype(jnp.float32)
    from_prev = shifted(ext_grad[span - count_atoms :].astype(jnp.bfloat16), "dom", 1).astype(
        jnp.float32
    )
    total = grad_own + ext_grad[count_atoms : count_atoms + count_atoms]
    total = total + from_next
    total = total + from_prev
    part_pair = jnp.dot(prod.T, dpre, preferred_element_type=jnp.float32)
    part_edge = jnp.dot(edges.T, dpre, preferred_element_type=jnp.float32)
    part_block = jnp.dot(act.T, dblock, preferred_element_type=jnp.float32)
    sum_pair, sum_edge, sum_block = lax.psum((part_pair, part_edge, part_block), ("dom", "slab"))
    scale = float(lax.axis_size("slab") * domains * pair_list.shape[1]) ** (-0.5)
    return (received[None], total[None], sum_pair * scale, sum_edge * scale, sum_block * scale)


def solution(mesh):
    in_specs = (
        P("slab", ("groups", "dom"), None),
        P("slab", ("groups", "dom")),
        P("slab", ("groups", "dom"), None),
        P("slab", ("groups", "dom"), None),
        P("slab", ("groups", "dom"), None),
        P("slab", ("groups", "dom"), None),
        P(),
        P(),
        P(),
    )
    out_specs = (
        P("slab", ("groups", "dom"), None),
        P("slab", ("groups", "dom"), None),
        P("groups", None),
        P("groups", None),
        P("groups", None),
    )
    return jax.shard_map(shards, mesh=mesh, in_specs=in_specs, out_specs=out_specs, check_vma=False)
```

profile of v0, /device:TPU:1, one launch (start us, length us, event | category | flops | bytes accessed | tf_op | source)
XLA Modules:
  0.0 220.2 jit_solution(17698270814433174487)
XLA Ops:
  7.2 0.7 convert_element_type.58
  7.9 5.1 %collective-permute-start.1 = (bf16[1,128]{1,0:T(2,128)(2,1)S(1)}, bf16[1,128]{1,0:T(2,128)(2,1)S(1)}, u32[]{:S(2)}, u32[]{:S(2)}) collective-permute-start(bf16[1,128]{1,0:T(2,128)(2,1)S(1)} %convert_element_type.58), channel_id=1, source_target_pairs={{2,0},{4,2},{6,4},{8,6},{10,8},{12,10},{14,12},{0,14},{3,1},{5,3},... | collective-permute-start | bytes 776 | tf_op jit(solution)/shard_map/ppermute | solution.py:18
  13.0 4.2 %collective-permute-start.4 = (bf16[1,128,512]{2,1,0:T(8,128)(2,1)}, bf16[1,128,512]{2,1,0:T(8,128)(2,1)S(1)}, u32[]{:S(2)}, u32[]{:S(2)}) collective-permute-start(bf16[1,128,512]{2,1,0:T(8,128)(2,1)} %param.9), channel_id=1, source_target_pairs={{2,0},{4,2},{6,4},{8,6},{10,8},{12,10},{14,12},{0,14},{3,1},{5,3},... | collective-permute-start | bytes 393224 | tf_op jit(solution)/shard_map/ppermute | solution.py:18
  17.2 1.4 copy.35
  18.6 0.1 slice_bitcast_fusion
  18.8 1.1 copy.30
  19.9 4.2 %all-to-all-start.1 = ((bf16[8,384,169]{1,2,0:T(8,128)(2,1)}), bf16[8,384,169]{1,2,0:T(8,128)(2,1)}, u32[]{:S(2)}, u32[]{:S(2)}) async-start(bf16[8,384,169]{1,2,0:T(8,128)(2,1)} %copy.30), calls=%async_computation.1 | async-start | bytes 2162688 | tf_op jit(solution)/shard_map/all_to_all | solution.py:80
  24.3 2.3 %reduce-window.6 = s32[8,16,128]{2,1,0:T(8,128)S(1)} reduce-window(s32[8,16,128]{2,1,0:T(8,128)S(1)} %fusion.28, s32[]{:T(128)} %constant.53.clone.1), window={size=1x1x128 pad=0_0x0_0x127_0}, to_apply=%region_0.1 | reduce-window | flops 2080768 | bytes 131076 | tf_op jit(solution)/shard_map/reduce-window
  26.6 0.3 slice_reduce_fusion
  26.9 0.2 reduce-window.9
  27.3 1.0 convolution_convert_fusion
  28.4 1.6 collective-permute-start.5
  30.0 0.1 collective-permute-start.2
  30.1 12.6 %gather_fusion = s32[2048]{0:T(1024)S(1)} fusion(s32[128]{0:T(128)S(1)} %bitcast.77, s32[2048]{0:T(1024)S(1)} %broadcast_clamp_fusion.2), kind=kCustom, calls=%fused_computation | custom fusion | bytes 24576 | tf_op jit(solution)/shard_map/gather | solution.py:61
  42.8 13.1 %gather_fusion.1 = bf16[2048]{0:T(1024)(128)(2,1)S(1)} fusion(bf16[768]{0:T(1024)(128)(2,1)S(1)} %pad_maximum_fusion, s32[2048]{0:T(1024)S(1)} %broadcast_clamp_fusion.1), kind=kCustom, calls=%fused_computation.1 | custom fusion | bytes 16384 | tf_op jit(solution)/shard_map/gather | solution.py:62
  55.9 2.1 fusion.6
  58.1 1.3 fusion.11
  59.4 3.2 %multiply_convert_fusion.1 = (bf16[2048,512]{1,0:T(8,128)(2,1)S(1)}, f32[2048,512]{1,0:T(8,128)}) fusion(f32[2048,512]{1,0:T(8,128)S(1)} %fusion.11, bf16[128,512]{1,0:T(8,128)(2,1)S(1)} %copy-done.19, bf16[1,2048,128]{2,1,0:T(8,128)(2,1)S(1)} %copy-done), kind=kOutput, calls=%fused_computation.13 | convolution fusion | flops 274726912 | bytes 11141120 | tf_op jit(solution)/shard_map/dot_general | solution.py:65
  62.6 1.3 copy-done.20
  64.0 0.8 fusion.7
  64.8 0.5 copy.27
  65.4 9.8 %scatter_custom_fusion = bf16[3072,169]{1,0:T(8,128)(2,1)S(1)} fusion(s32[2048]{0:T(1024)S(1)} %bitcast.90, bf16[2048,169]{1,0:T(8,128)(2,1)S(1)} %copy.27, bf16[]{:T(256)} %constant.34.clone.1), kind=kCustom, calls=%fused_computation.34 | custom fusion | bytes 1038338 | tf_op jit(solution)/shard_map/scatter | solution.py:78
  75.1 1.5 copy.28
  76.6 5.6 %all-to-all-start = ((bf16[8,384,169]{1,2,0:T(8,128)(2,1)}), bf16[8,384,169]{1,2,0:T(8,128)(2,1)}, u32[]{:S(2)}, u32[]{:S(2)}) async-start(bf16[8,384,169]{1,2,0:T(8,128)(2,1)} %copy.28), calls=%async_computation | async-start | bytes 2162688 | tf_op jit(solution)/shard_map/all_to_all | solution.py:79
  82.3 1.6 copy.31
  83.9 7.5 %gather_fusion.2 = bf16[2048,169]{1,0:T(8,128)(2,1)S(1)} fusion(bf16[3072,169]{1,0:T(8,128)(2,1)S(1)} %bitcast.78, s32[2048]{0:T(1024)S(1)} %broadcast_clamp_fusion), kind=kCustom, calls=%fused_computation.2 | custom fusion | bytes 1392640 | tf_op jit(solution)/shard_map/gather | solution.py:81
  91.4 0.7 copy.32
  92.1 4.4 %multiply_convert_fusion = bf16[2048,512]{1,0:T(8,128)(2,1)S(1)} fusion(f32[2048,512]{1,0:T(8,128)} %get-tuple-element.40, bf16[512,169]{0,1:T(8,128)(2,1)S(1)} %copy-done.18, bf16[2048,169]{0,1:T(8,128)(2,1)S(1)} %copy.32, s32[2048]{0:T(1024)S(1)} %convert_element_type.59, s32[2048]{0:T(1024)S(1)} %gather_fusion, s32[169]{0:T(256)S(1)} %get-tuple-element.41, ...), kind=kOutput, calls=%fused_computation.12 | convolution fusion | flops 365240320 | bytes 7174472 | tf_op jit(solution)/shard_map/dot_general | solution.py:83
  96.6 1.3 fusion.41
  97.9 0.3 copy-done.3
  98.2 5.7 %fusion = f32[768,512]{1,0:T(8,128)S(1)} fusion(f32[2048,512]{1,0:T(8,128)S(1)} %fusion.41, bf16[2048,512]{1,0:T(8,128)(2,1)S(1)} %copy-done.3, s32[2048]{0:T(1024)S(1)} %fusion.30), kind=kOutput, calls=%fused_computation.5 | convolution fusion | flops 9667346432 | bytes 7872512 | tf_op jit(solution)/shard_map/dot_general | solution.py:93
  104.0 0.8 collective-permute-start.6
  104.8 2.3 %fusion.9 = f32[512,512]{1,0:T(8,128)} fusion(bf16[2048,512]{1,0:T(8,128)(2,1)S(1)} %multiply_convert_fusion, bf16[2048,512]{1,0:T(8,128)(2,1)S(1)} %copy-done.5, bf16[2048,512]{1,0:T(8,128)(2,1)S(1)} %copy-done.3), kind=kOutput, calls=%fused_computation.27 | convolution fusion | flops 1077936128 | bytes 7340032 | tf_op jit(solution)/shard_map/dot_general | solution.py:108
  107.1 1.4 convolution_bitcast_fusion
  108.5 0.5 copy-done.21
  109.0 1.3 fusion.34
  110.3 1.4 fusion.37
  111.7 0.7 fusion.39
  112.4 4.4 %collective-permute-start.7 = (bf16[128,512]{1,0:T(8,128)(2,1)}, bf16[128,512]{1,0:T(8,128)(2,1)}, u32[]{:S(2)}, u32[]{:S(2)}) collective-permute-start(bf16[128,512]{1,0:T(8,128)(2,1)} %get-tuple-element.32), channel_id=1, source_target_pairs={{0,14},{2,0},{4,2},{6,4},{8,6},{10,8},{12,10},{14,12},{1,15},{3,1}... | collective-permute-start | bytes 393224 | tf_op jit(solution)/shard_map/ppermute | solution.py:31
  116.8 5.1 %fusion.3 = f32[128,512]{1,0:T(8,128)} fusion(f32[2048,512]{1,0:T(8,128)} %copy-done.6, bf16[2048,512]{1,0:T(8,128)(2,1)S(1)} %copy-done.5, s32[2048]{0:T(1024)S(1)} %bitcast.83), kind=kOutput, calls=%fused_computation.11 | convolution fusion | flops 1612972032 | bytes 6561792 | tf_op jit(solution)/shard_map/dot_general | solution.py:87
  122.0 1.5 copy.29
  123.5 1.5 broadcast_in_dim.18
  124.9 1.8 collective-permute-done.8
  126.7 1.7 fusion.24
  128.4 80.9 %all-reduce.3.cloned.1.call-done = (f32[512,512]{1,0:T(8,128)}, f32[128,512]{0,1:T(8,128)}, f32[512,169]{0,1:T(8,128)}) async-done(((f32[512,512]{1,0:T(8,128)}, f32[128,512]{0,1:T(8,128)}, f32[512,169]{0,1:T(8,128)}), (f32[512,512]{1,0:T(8,128)}, f32[128,512]{0,1:T(8,128)}, f32[512,169]{0,1:T(8,128)})) %all-reduce.3.cloned.1.call-update) | async-done | bytes 1656848 | tf_op jit(solution)/shard_map/psum | solution.py:111
  209.4 2.4 %broadcast_multiply_fusion = f32[512,512]{1,0:T(8,128)} fusion(f32[512,512]{1,0:T(8,128)} %get-tuple-element.25), kind=kLoop, calls=%fused_computation.38 | loop fusion | flops 262144 | bytes 2097152 | tf_op jit(solution)/shard_map/mul | solution.py:113
  211.8 0.8 copy.33
  212.6 0.8 broadcast_multiply_fusion.1
  (77 shorter events, 0.7 us)
Async XLA Ops:
  7.2 52.3 %copy-start = (bf16[1,2048,128]{2,1,0:T(8,128)(2,1)S(1)}, bf16[1,2048,128]{2,1,0:T(8,128)(2,1)}, u32[]{:S(2)}) copy-start(bf16[1,2048,128]{2,1,0:T(8,128)(2,1)} %param.13) | copy-start | bytes 1572868
  7.9 22.1 %collective-permute-start.1 = (bf16[1,128]{1,0:T(2,128)(2,1)S(1)}, bf16[1,128]{1,0:T(2,128)(2,1)S(1)}, u32[]{:S(2)}, u32[]{:S(2)}) collective-permute-start(bf16[1,128]{1,0:T(2,128)(2,1)S(1)} %convert_element_type.58), channel_id=1, source_target_pairs={{2,0},{4,2},{6,4},{8,6},{10,8},{12,10},{14,12},{0,14},{3,1},{5,3},... | collective-permute-start | bytes 776 | tf_op jit(solution)/shard_map/ppermute | solution.py:18
  13.0 17.0 %collective-permute-start = (bf16[1,128]{1,0:T(2,128)(2,1)S(1)}, bf16[1,128]{1,0:T(2,128)(2,1)S(1)}, u32[]{:S(2)}, u32[]{:S(2)}) collective-permute-start(bf16[1,128]{1,0:T(2,128)(2,1)S(1)} %convert_element_type.58), channel_id=1, source_target_pairs={{0,2},{2,4},{4,6},{6,8},{8,10},{10,12},{12,14},{14,0},{1,3},{3,5},... | collective-permute-start | bytes 776 | tf_op jit(solution)/shard_map/ppermute | solution.py:16
  13.0 15.3 %collective-permute-start.3 = (bf16[1,128,512]{2,1,0:T(8,128)(2,1)}, bf16[1,128,512]{2,1,0:T(8,128)(2,1)S(1)}, u32[]{:S(2)}, u32[]{:S(2)}) collective-permute-start(bf16[1,128,512]{2,1,0:T(8,128)(2,1)} %param.9), channel_id=1, source_target_pairs={{0,2},{2,4},{4,6},{6,8},{8,10},{10,12},{12,14},{14,0},{1,3},{3,5},... | collective-permute-start | bytes 393224 | tf_op jit(solution)/shard_map/ppermute | solution.py:16
  13.0 15.4 %collective-permute-start.4 = (bf16[1,128,512]{2,1,0:T(8,128)(2,1)}, bf16[1,128,512]{2,1,0:T(8,128)(2,1)S(1)}, u32[]{:S(2)}, u32[]{:S(2)}) collective-permute-start(bf16[1,128,512]{2,1,0:T(8,128)(2,1)} %param.9), channel_id=1, source_target_pairs={{2,0},{4,2},{6,4},{8,6},{10,8},{12,10},{14,12},{0,14},{3,1},{5,3},... | collective-permute-start | bytes 393224 | tf_op jit(solution)/shard_map/ppermute | solution.py:18
  18.7 5.4 %copy-start.17 = (s32[1,2048,2]{1,2,0:T(2,128)S(1)}, s32[1,2048,2]{1,2,0:T(2,128)}, u32[]{:S(2)}) copy-start(s32[1,2048,2]{1,2,0:T(2,128)} %param.11) | copy-start | bytes 49156
  18.8 5.6 %copy-start.16 = (s32[1,2048,1]{1,2,0:T(1,128)S(1)}, s32[1,2048,1]{1,2,0:T(1,128)}, u32[]{:S(2)}) copy-start(s32[1,2048,1]{1,2,0:T(1,128)} %param.12) | copy-start | bytes 24580
  18.8 8.5 %copy-start.13 = (bf16[1,128,512]{2,1,0:T(8,128)(2,1)S(1)}, bf16[1,128,512]{2,1,0:T(8,128)(2,1)}, u32[]{:S(2)}) copy-start(bf16[1,128,512]{2,1,0:T(8,128)(2,1)} %param.9) | copy-start | bytes 393220
  19.9 56.7 %all-to-all-start.1 = ((bf16[8,384,169]{1,2,0:T(8,128)(2,1)}), bf16[8,384,169]{1,2,0:T(8,128)(2,1)}, u32[]{:S(2)}, u32[]{:S(2)}) async-start(bf16[8,384,169]{1,2,0:T(8,128)(2,1)} %copy.30), calls=%async_computation.1 | async-start | bytes 2162688 | tf_op jit(solution)/shard_map/all_to_all | solution.py:80
  24.2 6.0 %copy-start.1 = (s32[1,128]{1,0:T(1,128)S(1)}, s32[1,128]{1,0:T(1,128)}, u32[]{:S(2)}) copy-start(s32[1,128]{1,0:T(1,128)} %param.10) | copy-start | bytes 1540
  28.3 29.7 %copy-start.2 = (bf16[2048,512]{1,0:T(8,128)(2,1)}, bf16[2048,512]{1,0:T(8,128)(2,1)S(1)}, u32[]{:S(2)}) copy-start(bf16[2048,512]{1,0:T(8,128)(2,1)S(1)} %convolution_convert_fusion) | copy-start | bytes 6291460
  28.4 27.5 %collective-permute-start.5 = (bf16[1,384,512]{2,1,0:T(8,128)(2,1)S(1)}, bf16[1,384,512]{2,1,0:T(8,128)(2,1)S(1)}, u32[]{:S(2)}, u32[]{:S(2)}) collective-permute-start(bf16[1,384,512]{2,1,0:T(8,128)(2,1)S(1)} %constant_dynamic-update-slice_fusion), channel_id=1, source_target_pairs={{0,1},{1,0},{2,3},{3,2},{4,5},{5,4},{6,7},{7,6},{8,9},{9,8},{10,11... | collective-permute-start | bytes 1179656 | tf_op jit(solution)/shard_map/ppermute | solution.py:26
  30.0 12.7 %collective-permute-start.2 = (bf16[1,384]{1,0:T(2,128)(2,1)S(1)}, bf16[1,384]{1,0:T(2,128)(2,1)S(1)}, u32[]{:S(2)}, u32[]{:S(2)}) collective-permute-start(bf16[1,384]{1,0:T(2,128)(2,1)S(1)} %get-tuple-element.31), channel_id=1, source_target_pairs={{0,1},{1,0},{2,3},{3,2},{4,5},{5,4},{6,7},{7,6},{8,9},{9,8},{10,11... | collective-permute-start | bytes 2312 | tf_op jit(solution)/shard_map/ppermute | solution.py:26
  55.9 2.1 copy-start.7
  58.1 1.4 copy-start.4
  58.1 1.4 copy-start.19
  59.4 4.6 %copy-start.18 = (bf16[512,169]{0,1:T(8,128)(2,1)S(1)}, bf16[512,169]{0,1:T(8,128)(2,1)}, u32[]{:S(2)}) copy-start(bf16[512,169]{0,1:T(8,128)(2,1)} %param.17) | copy-start | bytes 519172
  62.6 1.3 copy-start.20
  76.6 45.3 %all-to-all-start = ((bf16[8,384,169]{1,2,0:T(8,128)(2,1)}), bf16[8,384,169]{1,2,0:T(8,128)(2,1)}, u32[]{:S(2)}, u32[]{:S(2)}) async-start(bf16[8,384,169]{1,2,0:T(8,128)(2,1)} %copy.28), calls=%async_computation | async-start | bytes 2162688 | tf_op jit(solution)/shard_map/all_to_all | solution.py:79
  82.2 127.1 %all-reduce.3.cloned.1.call-start = ((), (), s32[]{:S(2)}) async-start(), calls=%async_computation.2 | async-start | bytes 3342336 | tf_op jit(solution)/shard_map/psum | solution.py:111
  92.1 4.5 %copy-start.11 = (bf16[2048,169]{0,1:T(8,128)(2,1)}, bf16[2048,169]{0,1:T(8,128)(2,1)S(1)}, u32[]{:S(2)}) copy-start(bf16[2048,169]{0,1:T(8,128)(2,1)S(1)} %copy.32) | copy-start | bytes 2076676
  92.1 4.5 %copy-start.8 = (bf16[512,512]{1,0:T(8,128)(2,1)S(1)}, bf16[512,512]{1,0:T(8,128)(2,1)}, u32[]{:S(2)}) copy-start(bf16[512,512]{1,0:T(8,128)(2,1)} %param.15) | copy-start | bytes 1572868
  96.6 1.6 copy-start.3
  98.2 5.7 %copy-start.6 = (f32[2048,512]{1,0:T(8,128)}, f32[2048,512]{1,0:T(8,128)S(1)}, u32[]{:S(2)}) copy-start(f32[2048,512]{1,0:T(8,128)S(1)} %fusion.41) | copy-start | bytes 12582916
  98.2 6.6 %copy-start.5 = (bf16[2048,512]{1,0:T(8,128)(2,1)S(1)}, bf16[2048,512]{1,0:T(8,128)(2,1)}, u32[]{:S(2)}) copy-start(bf16[2048,512]{1,0:T(8,128)(2,1)} %copy-done.4) | copy-start | bytes 6291460
  103.9 3.1 %copy-start.10 = (f32[768,512]{1,0:T(8,128)}, f32[768,512]{1,0:T(8,128)S(1)}, u32[]{:S(2)}) copy-start(f32[768,512]{1,0:T(8,128)S(1)} %fusion) | copy-start | bytes 4718596
  104.0 6.3 %collective-permute-start.6 = (bf16[384,512]{1,0:T(8,128)(2,1)S(1)}, bf16[384,512]{1,0:T(8,128)(2,1)}, u32[]{:S(2)}, u32[]{:S(2)}) collective-permute-start(bf16[384,512]{1,0:T(8,128)(2,1)S(1)} %slice.70), channel_id=1, source_target_pairs={{0,1},{1,0},{2,3},{3,2},{4,5},{5,4},{6,7},{7,6},{8,9},{9,8},{10,11... | collective-permute-start | bytes 1179656 | tf_op jit(solution)/shard_map/ppermute | solution.py:26
  107.0 1.5 copy-start.12
  107.1 1.9 copy-start.21
  112.4 12.5 %collective-permute-start.7 = (bf16[128,512]{1,0:T(8,128)(2,1)}, bf16[128,512]{1,0:T(8,128)(2,1)}, u32[]{:S(2)}, u32[]{:S(2)}) collective-permute-start(bf16[128,512]{1,0:T(8,128)(2,1)} %get-tuple-element.32), channel_id=1, source_target_pairs={{0,14},{2,0},{4,2},{6,4},{8,6},{10,8},{12,10},{14,12},{1,15},{3,1}... | collective-permute-start | bytes 393224 | tf_op jit(solution)/shard_map/ppermute | solution.py:31
  116.8 9.9 %collective-permute-start.8 = (bf16[128,512]{1,0:T(8,128)(2,1)S(1)}, bf16[128,512]{1,0:T(8,128)(2,1)}, u32[]{:S(2)}, u32[]{:S(2)}) collective-permute-start(bf16[128,512]{1,0:T(8,128)(2,1)S(1)} %get-tuple-element.33), channel_id=1, source_target_pairs={{0,2},{2,4},{4,6},{6,8},{8,10},{10,12},{12,14},{14,0},{1,3},{3,5},... | collective-permute-start | bytes 393224 | tf_op jit(solution)/shard_map/ppermute | solution.py:31
  121.9 4.7 %copy-start.9 = (f32[128,512]{1,0:T(8,128)S(1)}, f32[128,512]{1,0:T(8,128)}, u32[]{:S(2)}) copy-start(f32[128,512]{1,0:T(8,128)} %fusion.3) | copy-start | bytes 786436
  209.4 2.4 %copy-start.15 = (f32[128,512]{0,1:T(8,128)S(1)}, f32[128,512]{0,1:T(8,128)}, u32[]{:S(2)}) copy-start(f32[128,512]{0,1:T(8,128)} %get-tuple-element.26) | copy-start | bytes 786436
  209.4 3.2 %copy-start.14 = (f32[512,169]{0,1:T(8,128)S(1)}, f32[512,169]{0,1:T(8,128)}, u32[]{:S(2)}) copy-start(f32[512,169]{0,1:T(8,128)} %get-tuple-element.27) | copy-start | bytes 1038340
Sparse Core Ops, SparseCore 0:
  110.4 98.8 all-reduce.2
where the time goes:
time: 223 us; the launch traced here: 220 us
  waiting for transfers between devices  82.8 us (37%)
  local copies, waits for them, and re-layouts  57.1 us (26%)
  matrix products  30 us (13%)
  starting transfers between devices  26.1 us (12%)
  between operations  14.5 us (7%)
  other arithmetic  9.81 us (4%)
    psum x1, waiting for transfers between devices, shards(): lax.psum((part_pair, part_edge, part_block), ('dom', 'slab'))  80.9 us
    gather x1, local copies, waits for them, and re-layouts, shards(): n_near = table_count[near_idx].astype(jnp.int32)  13.1 us
    gather x1, local copies, waits for them, and re-layouts, shards(): n_own = orbitals[0][own_idx]  12.6 us
    scatter x1, local copies, waits for them, and re-layouts, shards(): jnp.zeros((domains * capacity, block_size), jnp.bfloat16).at[target]  9.78 us
    ppermute x2, starting transfers between devices, padded(): lax.ppermute(head, axis, [((i + 1) % count, i) for i in range(count)])  9.3 us
    gather x2, local copies, waits for them, and re-layouts, shards(): cot = returned[target]  8.17 us
    dot_general x1, matrix products, shards(): jnp.dot(near_hits.astype(jnp.float32).T, dprod * x_own.astype(jnp.float32...  5.71 us
    all_to_all x1, starting transfers between devices, shards(): lax.all_to_all(outgoing, 'dom', split_axis=0, concat_axis=0, tiled=True)  5.62 us
  transfers between devices with their start and end apart: 12, of which 2 were waited for; matrix products, arithmetic and copies ran while one was open for 41% of the time, Pallas kernels for 0%

commit v1 on v0

v1 whole, which is shorter than its diff:
```python
import functools

import jax
import jax.numpy as jnp
from jax import lax
from jax.experimental import pallas as pl
from jax.experimental.pallas import tpu as pltpu
from jax.sharding import PartitionSpec as P

ORB = 13
RIM = 32
LANE = 128
TILE = 256
F32 = jnp.float32
BF16 = jnp.bfloat16


def nn(a, b):
    return jnp.dot(a, b, preferred_element_type=F32)


def nt(a, b):
    return lax.dot_general(a, b, (((1,), (1,)), ((), ())), preferred_element_type=F32)


def tn(a, b):
    return lax.dot_general(a, b, (((0,), (0,)), ((), ())), preferred_element_type=F32)


def bits(cond):
    return jnp.where(cond, 1.0, 0.0).astype(BF16)


def iota(shape, dim):
    return lax.broadcasted_iota(jnp.int32, shape, dim)


def orbital_of(lanes):
    row = jnp.zeros_like(lanes)
    for k in range(1, 20):
        row = row + jnp.where(lanes >= ORB * k, 1, 0)
    return row.astype(F32), (lanes - ORB * row).astype(F32)


def kernel(
    D, C, T, A, FEAT, EDGE, BLOCK, PIECE, scale,
    feat_ref, orb_ref, pc_ref, oc_ref, rows_ref, edge_ref, cot_ref, wp_ref, we_ref, wb_ref,
    bo_ref, ag_ref, gp_ref, ge_ref, gb_ref,
    tab, wbp, cs, cr, bs, br, tr, tc, xo_s, xn_s, prod_s, act_s, ds_s, mask_s, blk, dc, cu,
    gt, gtb, gr, grp, gba, g32, gas, gar, hs, rb, fin,
    halo_s, halo_r, cot_s, cot_r, blk_s, blk_r, grad_s, grad_r, sum_s, sum_r, red_s, red_r,
    all_s, all_r, fwd_s, fwd_r,
):
    W = A + 2 * RIM
    C3 = C // 3
    S = D * C
    R = D * PIECE
    TAIL = BLOCK - LANE
    me = lax.axis_index("dom")
    slab = lax.axis_index("slab")
    other = 1 - slab
    nxt = lax.rem(me + 1, D)
    prv = lax.rem(me + D - 1, D)
    ntile = T // TILE

    def rcopy(src, dst, ssem, rsem, dom, layer):
        return pltpu.make_async_remote_copy(
            src_ref=src, dst_ref=dst, send_sem=ssem, recv_sem=rsem,
            device_id={"dom": dom, "slab": layer}, device_id_type=pl.DeviceIdType.MESH,
        )

    def peer(k):
        return lax.rem(me + k, D)

    def rows_at(t):
        return pl.ds(pl.multiple_of(t * TILE, TILE), TILE)

    barrier = pltpu.get_barrier_semaphore()

    @pl.loop(1, D)
    def _(k):
        pl.semaphore_signal(barrier, inc=1, device_id={"dom": peer(k), "slab": slab}, device_id_type=pl.DeviceIdType.MESH)

    for dom in (me, nxt, prv):
        pl.semaphore_signal(barrier, inc=1, device_id={"dom": dom, "slab": other}, device_id_type=pl.DeviceIdType.MESH)

    diag = jnp.where(iota((A, A), 0) == iota((A, A), 1), orb_ref[...].astype(F32), 0.0).astype(BF16)
    tab[RIM:RIM + A, 0:FEAT] = feat_ref[...]
    tab[RIM:RIM + A, FEAT:FEAT + LANE] = nn(diag, jnp.ones((A, LANE), BF16)).astype(BF16)
    pl.semaphore_wait(barrier, D + 2)

    head = tab.at[RIM:2 * RIM]
    tail = tab.at[A:A + RIM]
    halos = [
        rcopy(tail, tab.at[0:RIM], halo_s.at[0], halo_r.at[0], nxt, slab),
        rcopy(head, tab.at[RIM + A:W], halo_s.at[1], halo_r.at[1], prv, slab),
        rcopy(tail, tab.at[W:W + RIM], halo_s.at[2], halo_r.at[2], nxt, other),
        rcopy(head, tab.at[W + RIM + A:2 * W], halo_s.at[3], halo_r.at[3], prv, other),
        rcopy(tab.at[RIM:RIM + A], tab.at[W + RIM:W + RIM + A], halo_s.at[4], halo_r.at[4], me, other),
    ]
    for h in halos:
        h.start()

    def spread(g, height):
        return bits(iota((height, LANE), 0) + TAIL * g == iota((height, LANE), 1))

    def pack_cot(d, dst):
        base = pl.multiple_of(d * C, C)
        dst[d, 0:C, :] = cot_ref[pl.ds(base, C), 0:LANE]
        acc = None
        for g in range(3):
            part = nn(cot_ref[pl.ds(pl.multiple_of(base + g * C3, 16), C3), LANE:BLOCK], spread(g, TAIL))
            acc = part if acc is None else acc + part
        dst[d, C:C + C3, :] = acc.astype(BF16)

    def exchange(src, dst, ssem, rsem, d, at):
        return rcopy(src.at[d], dst.at[at], ssem.at[d], rsem.at[at], d, slab)

    @pl.loop(1, D)
    def _(k):
        d = peer(k)
        pack_cot(d, cs)
        exchange(cs, cr, cot_s, cot_r, d, me).start()

    pack_cot(me, cr)

    wbp[...] = jnp.zeros_like(wbp)
    wbp[:, 0:LANE] = wb_ref[:, 0:LANE]
    wbp[:, LANE:BLOCK] = wb_ref[:, LANE:BLOCK]

    DP = max(16, D)
    upper = bits(iota((TILE, TILE), 0) <= iota((TILE, TILE), 1))
    lower = bits(iota((TILE, TILE), 0) >= iota((TILE, TILE), 1))

    def slots(t, carry):
        down, across = carry
        at = rows_at(t)
        ow = rows_ref[2:3, at]
        hit = jnp.where(iota((DP, TILE), 0) == ow, 1.0, 0.0)
        rank = nn(hit.astype(BF16), upper) + down
        slot = jnp.sum(hit * rank, axis=0, keepdims=True) - 1.0
        tr[0:1, at] = ow * C + slot.astype(jnp.int32)
        oc = oc_ref[at, 0:1]
        hit_c = jnp.where(iota((TILE, LANE), 1) == oc, 1.0, 0.0)
        rank_c = nn(lower, hit_c.astype(BF16)) + across
        slot_c = jnp.sum(hit_c * rank_c, axis=1, keepdims=True) - 1.0
        tc[at, 0:1] = oc * C + slot_c.astype(jnp.int32)
        return down + jnp.sum(hit, axis=1, keepdims=True), across + jnp.sum(hit_c, axis=0, keepdims=True)

    lax.fori_loop(0, ntile, slots, (jnp.zeros((DP, 1), F32), jnp.zeros((1, LANE), F32)))

    for h in halos:
        h.wait_recv()

    def table_row(raw):
        return jnp.where(raw >= 3 * A, raw - 3 * A + W, raw) - (A - RIM)

    lane = iota((1, LANE), 1)
    div_hi, mod_hi = orbital_of(lane)
    div_lo, mod_lo = orbital_of(lane + LANE)

    @pl.loop(0, ntile)
    def _(t):
        at = rows_at(t)
        oh_own = bits(iota((TILE, A), 1) == pc_ref[at, 0:1])
        oh_near = bits(iota((TILE, 2 * W), 1) == table_row(pc_ref[at, 1:2]))
        xo = nn(oh_own, tab[RIM:RIM + A, :])
        xn = nn(oh_near, tab[...])
        xo_s[at, :] = xo[:, 0:FEAT].astype(BF16)
        xn_s[at, :] = xn[:, 0:FEAT].astype(BF16)
        prod = (xo[:, 0:FEAT] * xn[:, 0:FEAT]).astype(BF16)
        prod_s[at, :] = prod
        pre = nn(prod, wp_ref[...]) + nn(edge_ref[at, :], we_ref[...])
        sg = jax.nn.sigmoid(pre)
        act = (pre * sg).astype(BF16)
        act_s[at, :] = act
        ds_s[at, :] = sg * (1.0 + pre * (1.0 - sg))
        raw = nn(act, wbp[...])
        no, near = xo[:, FEAT:FEAT + LANE], xn[:, FEAT:FEAT + LANE]
        for i, (div, mod) in enumerate(((div_hi, mod_hi), (div_lo, mod_lo))):
            keep = (div < no) & (mod < near)
            mask_s[at, i * LANE:(i + 1) * LANE] = bits(keep)
            blk[at, i * LANE:(i + 1) * LANE] = jnp.where(keep, raw[:, i * LANE:(i + 1) * LANE], 0.0).astype(BF16)

    def pack_blocks(d, dst):
        acc = jnp.zeros((C, 2 * LANE), F32)
        step = 2 * TILE
        for j in range(T // step):
            hit = bits(iota((C, step), 0) + d * C == tr[0:1, j * step:(j + 1) * step])
            acc = acc + nn(hit, blk[j * step:(j + 1) * step, :])
        dst[d, 0:C, :] = acc[:, 0:LANE].astype(BF16)
        low = acc[:, LANE:2 * LANE].astype(BF16)
        packed = None
        for g in range(3):
            part = nn(low[g * C3:(g + 1) * C3, :], spread(g, LANE))
            packed = part if packed is None else packed + part
        dst[d, C:C + C3, :] = packed.astype(BF16)

    @pl.loop(1, D)
    def _(k):
        d = peer(k)
        pack_blocks(d, bs)
        exchange(bs, br, blk_s, blk_r, d, me).start()

    pack_blocks(me, br)

    def pick(g):
        row, col = iota((LANE, LANE), 0), iota((LANE, LANE), 1)
        return bits((row == col + TAIL * g) & (col < TAIL))

    dc[...] = jnp.zeros_like(dc)

    def collect(d):
        cu[:, 0:LANE] = cr[d, 0:C, :]
        packed = cr[d, C:C + C3, :]
        for g in range(3):
            cu[g * C3:(g + 1) * C3, LANE:2 * LANE] = nn(packed, pick(g)).astype(BF16)
        for t in range(ntile):
            at = slice(t * TILE, (t + 1) * TILE)
            hit = bits(iota((TILE, C), 1) + d * C == tc[at, 0:1])
            dc[at, :] += nn(hit, cu[...])

    collect(me)

    @pl.loop(1, D)
    def _(k):
        d = lax.rem(me + D - k, D)
        exchange(cs, cr, cot_s, cot_r, d, d).wait_recv()
        collect(d)

    gt[...] = jnp.zeros_like(gt)
    gp_ref[...] = jnp.zeros_like(gp_ref)
    ge_ref[...] = jnp.zeros_like(ge_ref)
    gba[...] = jnp.zeros_like(gba)

    @pl.loop(0, ntile)
    def _(t):
        at = rows_at(t)
        dblock = (dc[at, :] * mask_s[at, :].astype(F32)).astype(BF16)
        dact = nt(dblock, wbp[...])
        dpre = (dact * ds_s[at, :]).astype(BF16)
        gp_ref[...] += tn(prod_s[at, :], dpre)
        ge_ref[...] += tn(edge_ref[at, :], dpre)
        gba[...] += tn(act_s[at, :], dblock)
        dprod = nt(dpre, wp_ref[...])
        to_own = (dprod * xn_s[at, :].astype(F32)).astype(BF16)
        to_near = (dprod * xo_s[at, :].astype(F32)).astype(BF16)
        near_hit = bits(iota((2 * W, TILE), 0) == table_row(rows_ref[1:2, at]))
        own_hit = bits(iota((A, TILE), 0) == rows_ref[0:1, at])
        gt[...] += nn(near_hit, to_near)
        gt[RIM:RIM + A, :] += nn(own_hit, to_own)

    if 2 * R > 4 * FEAT + 4 * EDGE + 2 * FEAT:
        g32[...] = jnp.zeros_like(g32)
    for c in range(4):
        g32[c * FEAT:(c + 1) * FEAT, :] = gp_ref[:, c * LANE:(c + 1) * LANE]
        g32[4 * FEAT + c * EDGE:4 * FEAT + (c + 1) * EDGE, :] = ge_ref[:, c * LANE:(c + 1) * LANE]
    low = 4 * FEAT + 4 * EDGE
    for c in range(2):
        g32[low + c * FEAT:low + (c + 1) * FEAT, :] = gba[:, c * LANE:(c + 1) * LANE]
    gas[...] = g32[pl.ds(pl.multiple_of(other * R, 16), R), :].astype(BF16)
    swap = rcopy(gas, gar, sum_s, sum_r, me, other)
    swap.start()

    gtb[...] = gt[...].astype(BF16)
    grads = [
        rcopy(gtb.at[0:RIM], gr.at[0], grad_s.at[0], grad_r.at[0], prv, slab),
        rcopy(gtb.at[RIM + A:W], gr.at[1], grad_s.at[1], grad_r.at[1], nxt, slab),
        rcopy(gtb.at[W:W + RIM], gr.at[2], grad_s.at[2], grad_r.at[2], prv, other),
        rcopy(gtb.at[W + RIM + A:2 * W], gr.at[3], grad_s.at[3], grad_r.at[3], nxt, other),
        rcopy(gtb.at[W + RIM:W + RIM + A], grp, grad_s.at[4], grad_r.at[4], me, other),
    ]
    for g in grads:
        g.start()

    swap.wait_recv()
    hs[...] = (g32[pl.ds(pl.multiple_of(slab * R, 16), R), :] + gar[...].astype(F32)).astype(BF16)

    def piece(d, of=0):
        return pl.ds(pl.multiple_of(of * R + d * PIECE, 16), PIECE)

    def reduce_copy(d, at):
        return rcopy(hs.at[piece(d)], rb.at[at], red_s.at[d], red_r.at[at], d, slab)

    @pl.loop(1, D)
    def _(k):
        reduce_copy(peer(k), me).start()

    for g in grads:
        g.wait_recv()
    ag_ref[...] = gt[RIM:RIM + A, :] + grp[...].astype(F32)
    ag_ref[A - RIM:A, :] += gr[0].astype(F32) + gr[2].astype(F32)
    ag_ref[0:RIM, :] += gr[1].astype(F32) + gr[3].astype(F32)

    def add_up(k, total):
        s = lax.rem(me + D - k, D)
        reduce_copy(s, s).wait_recv()
        return total + rb[s].astype(F32)

    total = lax.fori_loop(1, D, add_up, g32[piece(me, slab), :] + gar[piece(me), :].astype(F32))
    fin[piece(me, slab), :] = total.astype(BF16)

    def gather_copy(d, at):
        return rcopy(fin.at[piece(at, slab)], fin.at[piece(at, slab)], all_s.at[d], all_r.at[at], d, slab)

    def forward_copy(s, of):
        return rcopy(fin.at[piece(s, of)], fin.at[piece(s, of)], fwd_s.at[s], fwd_r.at[s], me, other)

    @pl.loop(1, D)
    def _(k):
        gather_copy(peer(k), me).start()

    forward_copy(me, slab).start()

    def unpack(d):
        base = d * C
        bo_ref[pl.ds(pl.multiple_of(base, 16), C), 0:LANE] = br[d, 0:C, :]
        packed = br[d, C:C + C3, :]
        for g in range(3):
            part = nn(packed, pick(g)).astype(BF16)
            bo_ref[pl.ds(pl.multiple_of(base + g * C3, 16), C3), LANE:BLOCK] = part[:, 0:TAIL]

    unpack(me)

    @pl.loop(1, D)
    def _(k):
        d = lax.rem(me + D - k, D)
        exchange(bs, br, blk_s, blk_r, d, d).wait_recv()
        unpack(d)

    @pl.loop(1, D)
    def _(k):
        s = lax.rem(me + D - k, D)
        gather_copy(s, s).wait_recv()
        forward_copy(s, slab).start()

    @pl.loop(0, D)
    def _(s):
        forward_copy(s, other).wait_recv()

    for c in range(4):
        gp_ref[:, c * LANE:(c + 1) * LANE] = fin[c * FEAT:(c + 1) * FEAT, :].astype(F32) * scale
        ge_ref[:, c * LANE:(c + 1) * LANE] = fin[4 * FEAT + c * EDGE:4 * FEAT + (c + 1) * EDGE, :].astype(F32) * scale
    gb_ref[:, 0:LANE] = fin[low:low + FEAT, :].astype(F32) * scale
    gb_ref[:, LANE:BLOCK] = fin[low + FEAT:low + 2 * FEAT, 0:TAIL].astype(F32) * scale

    for h in halos + grads + [swap]:
        h.wait_send()

    @pl.loop(1, D)
    def _(k):
        d = peer(k)
        exchange(cs, cr, cot_s, cot_r, d, me).wait_send()
        exchange(bs, br, blk_s, blk_r, d, me).wait_send()
        reduce_copy(d, me).wait_send()
        gather_copy(d, me).wait_send()

    @pl.loop(0, D)
    def _(s):
        forward_copy(s, slab).wait_send()


def shards(features, orbitals, pair_list, owners, edge_feats, cotangent, w_pair, w_edge, w_block):
    A, FEAT = features.shape[1:]
    T = pair_list.shape[1]
    D = lax.axis_size("dom")
    S, BLOCK = cotangent.shape[1:]
    EDGE = edge_feats.shape[2]
    C = S // D
    W = A + 2 * RIM
    flat = 4 * FEAT + 4 * EDGE + 2 * FEAT
    PIECE = -(-flat // (2 * D * 16)) * 16
    R = D * PIECE
    scale = float(lax.axis_size("slab") * D * T) ** (-0.5)
    rows = jnp.concatenate([pair_list[0], owners[0]], axis=1).T
    row_len = C + C // 3
    dma = pltpu.SemaphoreType.DMA
    vmem = pl.BlockSpec(memory_space=pltpu.VMEM)
    outs = pl.pallas_call(
        functools.partial(kernel, D, C, T, A, FEAT, EDGE, BLOCK, PIECE, scale),
        out_shape=(
            jax.ShapeDtypeStruct((S, BLOCK), BF16),
            jax.ShapeDtypeStruct((A, FEAT), F32),
            jax.ShapeDtypeStruct((FEAT, FEAT), F32),
            jax.ShapeDtypeStruct((EDGE, FEAT), F32),
            jax.ShapeDtypeStruct((FEAT, BLOCK), F32),
        ),
        in_specs=[vmem] * 10,
        out_specs=(vmem,) * 5,
        scratch_shapes=[
            pltpu.VMEM((2 * W, FEAT + LANE), BF16),
            pltpu.VMEM((FEAT, 2 * LANE), BF16),
            pltpu.VMEM((D, row_len, LANE), BF16),
            pltpu.VMEM((D, row_len, LANE), BF16),
            pltpu.VMEM((D, row_len, LANE), BF16),
            pltpu.VMEM((D, row_len, LANE), BF16),
            pltpu.VMEM((8, T), jnp.int32),
            pltpu.VMEM((T, 1), jnp.int32),
            pltpu.VMEM((T, FEAT), BF16),
            pltpu.VMEM((T, FEAT), BF16),
            pltpu.VMEM((T, FEAT), BF16),
            pltpu.VMEM((T, FEAT), BF16),
            pltpu.VMEM((T, FEAT), F32),
            pltpu.VMEM((T, 2 * LANE), BF16),
            pltpu.VMEM((T, 2 * LANE), BF16),
            pltpu.VMEM((T, 2 * LANE), F32),
            pltpu.VMEM((C, 2 * LANE), BF16),
            pltpu.VMEM((2 * W, FEAT), F32),
            pltpu.VMEM((2 * W, FEAT), BF16),
            pltpu.VMEM((4, RIM, FEAT), BF16),
            pltpu.VMEM((A, FEAT), BF16),
            pltpu.VMEM((FEAT, 2 * LANE), F32),
            pltpu.VMEM((2 * R, LANE), F32),
            pltpu.VMEM((R, LANE), BF16),
            pltpu.VMEM((R, LANE), BF16),
            pltpu.VMEM((R, LANE), BF16),
            pltpu.VMEM((D, PIECE, LANE), BF16),
            pltpu.VMEM((2 * R, LANE), BF16),
            dma((5,)), dma((5,)), dma((D,)), dma((D,)), dma((D,)), dma((D,)), dma((5,)), dma((5,)),
            dma, dma, dma((D,)), dma((D,)), dma((D,)), dma((D,)), dma((D,)), dma((D,)),
        ],
        compiler_params=pltpu.CompilerParams(
            collective_id=0, has_side_effects=True, vmem_limit_bytes=56 * 1024 * 1024
        ),
        cost_estimate=pl.CostEstimate(flops=15 * 10**9, bytes_accessed=10**7, transcendentals=T * FEAT),
    )(features[0], orbitals, pair_list[0], owners[0], rows, edge_feats[0], cotangent[0], w_pair, w_edge, w_block)
    return (outs[0][None], outs[1][None], *outs[2:])


def solution(mesh):
    spread = P("slab", ("groups", "dom"), None)
    in_specs = (spread, P("slab", ("groups", "dom")), spread, spread, spread, spread, P(), P(), P())
    out_specs = (spread, spread, P("groups", None), P("groups", None), P("groups", None))
    return jax.shard_map(shards, mesh=mesh, in_specs=in_specs, out_specs=out_specs, check_vma=False)
```

time: 223 us -> 96.3 us (0.43)
  the two profiles are of different devices: /device:TPU:1 before, /device:TPU:25 now
where the time goes in v1:
time: 96.3 us; the launch traced here: 95.9 us
  Pallas kernels  81.2 us (84%)
  local copies, waits for them, and re-layouts  12.6 us (13%)
  other arithmetic  1.46 us (2%)
    pallas_call x1, Pallas kernels, shards(): pl.pallas_call(functools.partial(kernel, D, C, T, A, FEAT, EDGE, BLOCK, P...  81.2 us
    unnamed x19, local copies, waits for them, and re-layouts  9.2 us
    squeeze x1, local copies, waits for them, and re-layouts, shards(): pair_list[0]  2.06 us

profile of v1, /device:TPU:25, one launch (start us, length us, event | category | flops | bytes accessed | tf_op | source)
XLA Modules:
  0.0 95.9 jit_solution(16651638228020364023)
XLA Ops:
  0.6 0.0 copy-start
  0.6 0.0 copy-start.5
  0.7 1.5 %add_bitcast_fusion.rows_ref = s32[3,2048]{1,0:T(4,128)} fusion(s32[2048,1]{0,1:T(1,128)} %bitcast.14, s32[2048,2]{0,1:T(2,128)} %bitcast.12), kind=kLoop, calls=%fused_computation | loop fusion | flops 6144 | bytes 49152 | tf_op jit(solution)/shard_map/transpose | solution.py:375
  2.1 1.8 %copy.17.wb_ref = bf16[512,169]{1,0:T(8,128)(2,1)} copy(bf16[512,169]{0,1:T(8,128)(2,1)} %param.17) | data formatting | bytes 346112 | tf_op args[8]
  3.9 2.1 %copy.15.pc_ref = s32[2048,2]{1,0:T(8,128)} copy(s32[2048,2]{0,1:T(2,128)} %bitcast.13) | data formatting | bytes 32768 | tf_op jit(solution)/shard_map/squeeze | solution.py:426
  5.9 0.0 copy-done.5
  5.9 1.3 %copy.16.oc_ref = s32[2048,1]{1,0:T(8,128)} copy(s32[2048,1]{0,1:T(1,128)S(1)} %bitcast.15) | data formatting | bytes 16384 | tf_op jit(solution)/shard_map/squeeze | solution.py:426
  7.3 0.0 copy-done
  7.3 1.5 %copy.14 = bf16[1,3072,169]{2,1,0:T(8,128)(2,1)} copy(bf16[1,3072,169]{1,2,0:T(8,128)(2,1)S(1)} %copy-done) | data formatting | bytes 2076672 | tf_op args[5]
  8.8 81.2 %shard_map.128 = (bf16[3072,169]{1,0:T(8,128)(2,1)}, f32[128,512]{1,0:T(8,128)}, f32[512,512]{1,0:T(8,128)}, f32[128,512]{1,0:T(8,128)}, f32[512,169]{1,0:T(8,128)}) custom-call(bf16[128,512]{1,0:T(8,128)(2,1)} %bitcast.17, s32[1,128]{1,0:T(1,128)} %orb_ref.1, s32[2048,2]{1,0:T(8,128)} %copy.15.pc_ref, s32[2048,1]{1,0:T(8,128)} %copy.16.oc_ref, ...), custom_call_target="tpu_custom_call" | custom-call | flops 15000000512 | bytes 10000000 | tf_op jit(solution)/shard_map/pallas_call | solution.py:379
  90.0 0.0 copy-start.2
  90.0 0.0 copy-start.4
  90.0 0.0 copy-start.1
  90.0 2.6 %copy.18 = bf16[1,3072,169]{1,2,0:T(8,128)(2,1)} copy(bf16[1,3072,169]{2,1,0:T(8,128)(2,1)} %bitcast.9) | data formatting | bytes 2076672
  92.6 0.0 copy-done.2
  92.6 0.0 copy-start.3
  92.6 0.9 copy.19
  93.6 0.0 copy-done.4
  93.6 0.7 copy.23
  94.3 0.0 copy-done.1
  94.3 1.0 %copy.24 = f32[512,512]{1,0:T(8,128)} copy(f32[512,512]{1,0:T(8,128)S(1)} %copy-done.1) | data formatting | bytes 2097152
  95.2 0.0 copy-done.3
  95.2 0.7 copy.25
Async XLA Ops:
  0.6 6.6 %copy-start = (bf16[1,3072,169]{1,2,0:T(8,128)(2,1)S(1)}, bf16[1,3072,169]{1,2,0:T(8,128)(2,1)}, u32[]{:S(2)}) copy-start(bf16[1,3072,169]{1,2,0:T(8,128)(2,1)} %param.14) | copy-start | bytes 3115012
  0.6 5.3 %copy-start.5 = (s32[1,2048,1]{1,2,0:T(1,128)S(1)}, s32[1,2048,1]{1,2,0:T(1,128)}, u32[]{:S(2)}) copy-start(s32[1,2048,1]{1,2,0:T(1,128)} %param.12) | copy-start | bytes 24580
  90.0 2.6 %copy-start.2 = (f32[512,169]{1,0:T(8,128)S(1)}, f32[512,169]{1,0:T(8,128)}, u32[]{:S(2)}) copy-start(f32[512,169]{1,0:T(8,128)} %get-tuple-element.19) | copy-start | bytes 1038340
  90.0 3.5 %copy-start.4 = (f32[128,512]{1,0:T(8,128)S(1)}, f32[128,512]{1,0:T(8,128)}, u32[]{:S(2)}) copy-start(f32[128,512]{1,0:T(8,128)} %get-tuple-element.11) | copy-start | bytes 786436
  90.0 4.2 %copy-start.1 = (f32[512,512]{1,0:T(8,128)S(1)}, f32[512,512]{1,0:T(8,128)}, u32[]{:S(2)}) copy-start(f32[512,512]{1,0:T(8,128)} %get-tuple-element.27) | copy-start | bytes 3145732
  92.6 2.6 %copy-start.3 = (f32[128,512]{1,0:T(8,128)S(1)}, f32[128,512]{1,0:T(8,128)}, u32[]{:S(2)}) copy-start(f32[128,512]{1,0:T(8,128)} %get-tuple-element.28) | copy-start | bytes 786436

commit v2 on v1

v2 whole, which is shorter than its diff:
```python
import functools

import jax
import jax.numpy as jnp
from jax import lax
from jax.experimental import pallas as pl
from jax.experimental.pallas import tpu as pltpu
from jax.sharding import PartitionSpec as P

ORB = 13
RIM = 32
LANE = 128
TILE = 256
F32 = jnp.float32
BF16 = jnp.bfloat16


def nn(a, b):
    return jnp.dot(a, b, preferred_element_type=F32)


def nt(a, b):
    return lax.dot_general(a, b, (((1,), (1,)), ((), ())), preferred_element_type=F32)


def tn(a, b):
    return lax.dot_general(a, b, (((0,), (0,)), ((), ())), preferred_element_type=F32)


def bits(cond):
    return jnp.where(cond, 1.0, 0.0).astype(BF16)


def iota(shape, dim):
    return lax.broadcasted_iota(jnp.int32, shape, dim)


def orbital_of(lanes):
    row = jnp.zeros_like(lanes)
    for k in range(1, 20):
        row = row + jnp.where(lanes >= ORB * k, 1, 0)
    return row.astype(F32), (lanes - ORB * row).astype(F32)


def kernel(
    D, C, T, A, FEAT, EDGE, BLOCK, PIECE, scale,
    feat_ref, orb_ref, pair_ref, own_ref, edge_ref, cot_ref, wp_ref, we_ref, wb_ref,
    bo_ref, ag_ref, gp_ref, ge_ref, gb_ref,
    tab, wbp, cs, cr, bs, br, vr, vc, xo_s, xn_s, prod_s, act_s, ds_s, mask_s, blk, dc,
    gt, gtb, gr, grp, gba, g32, gas, gar, hs, rb, fin,
    halo_s, halo_r, cot_s, cot_r, blk_s, blk_r, grad_s, grad_r, sum_s, sum_r, red_s, red_r,
    all_s, all_r, fwd_s, fwd_r,
):
    W = A + 2 * RIM
    FULL = wbp.shape[0]
    CUT = FULL - 16
    R = D * PIECE
    me = lax.axis_index("dom")
    slab = lax.axis_index("slab")
    other = 1 - slab
    nxt = lax.rem(me + 1, D)
    prv = lax.rem(me + D - 1, D)
    ntile = T // TILE

    def rcopy(src, dst, ssem, rsem, dom, layer):
        return pltpu.make_async_remote_copy(
            src_ref=src, dst_ref=dst, send_sem=ssem, recv_sem=rsem,
            device_id={"dom": dom, "slab": layer}, device_id_type=pl.DeviceIdType.MESH,
        )

    def peer(k):
        i = k - 1
        return lax.rem(me + D // 2 + (1 - 2 * (i % 2)) * ((i + 1) // 2), D)

    def source(k):
        i = k - 1
        return lax.rem(me + 2 * D - D // 2 - (1 - 2 * (i % 2)) * ((i + 1) // 2), D)

    def rows_at(t):
        return pl.ds(pl.multiple_of(t * TILE, TILE), TILE)

    barrier = pltpu.get_barrier_semaphore()

    @pl.loop(1, D)
    def _(k):
        pl.semaphore_signal(barrier, inc=1, device_id={"dom": peer(k), "slab": slab}, device_id_type=pl.DeviceIdType.MESH)

    for dom in (me, nxt, prv):
        pl.semaphore_signal(barrier, inc=1, device_id={"dom": dom, "slab": other}, device_id_type=pl.DeviceIdType.MESH)

    diag = jnp.where(iota((A, A), 0) == iota((A, A), 1), orb_ref[...].astype(F32), 0.0).astype(BF16)
    tab[RIM:RIM + A, 0:FEAT] = feat_ref[...]
    tab[RIM:RIM + A, FEAT:FEAT + LANE] = nn(diag, jnp.ones((A, LANE), BF16)).astype(BF16)
    pl.semaphore_wait(barrier, D + 2)

    head = tab.at[RIM:2 * RIM]
    tail = tab.at[A:A + RIM]
    halos = [
        rcopy(tail, tab.at[0:RIM], halo_s.at[0], halo_r.at[0], nxt, slab),
        rcopy(head, tab.at[RIM + A:W], halo_s.at[1], halo_r.at[1], prv, slab),
        rcopy(tail, tab.at[W:W + RIM], halo_s.at[2], halo_r.at[2], nxt, other),
        rcopy(head, tab.at[W + RIM + A:2 * W], halo_s.at[3], halo_r.at[3], prv, other),
        rcopy(tab.at[RIM:RIM + A], tab.at[W + RIM:W + RIM + A], halo_s.at[4], halo_r.at[4], me, other),
    ]
    for h in halos:
        h.start()

    cs[:, CUT:FULL, :] = jnp.zeros((D, 16, C), BF16)
    cr[me, CUT:FULL, :] = jnp.zeros((16, C), BF16)

    def take_cot(d, dst):
        at = pl.ds(pl.multiple_of(d * C, C), C)
        dst[d, 0:CUT, :] = cot_ref[0:CUT, at]
        dst[d, CUT:BLOCK, :] = cot_ref[CUT:BLOCK, at]

    def exchange(src, dst, ssem, rsem, d, at):
        return rcopy(src.at[d], dst.at[at], ssem.at[d], rsem.at[at], d, slab)

    @pl.loop(1, D)
    def _(k):
        d = peer(k)
        take_cot(d, cs)
        exchange(cs, cr, cot_s, cot_r, d, me).start()

    take_cot(me, cr)

    wbp[CUT:FULL, :] = jnp.zeros((16, FEAT), BF16)
    wbp[0:CUT, :] = wb_ref[0:CUT, :]
    wbp[CUT:BLOCK, :] = wb_ref[CUT:BLOCK, :]

    def table_row(raw):
        return jnp.where(raw >= 3 * A, raw - 3 * A + W, raw) - (A - RIM)

    DP = max(16, D)
    upper = bits(iota((TILE, TILE), 0) <= iota((TILE, TILE), 1))
    down = jnp.zeros((DP, 1), F32)
    vr[0:1, :] = pair_ref[0:1, :].astype(F32)
    vr[1:2, :] = table_row(pair_ref[1:2, :]).astype(F32)
    vr[3:8, :] = jnp.zeros((5, T), F32)
    for t in range(ntile):
        at = slice(t * TILE, (t + 1) * TILE)
        ow = own_ref[0:1, at]
        hit = jnp.where(iota((DP, TILE), 0) == ow, 1.0, 0.0)
        rank = nn(hit.astype(BF16), upper) + down
        slot = jnp.sum(hit * rank, axis=0, keepdims=True) - 1.0
        vr[2:3, at] = (ow * C).astype(F32) + slot
        down = down + jnp.sum(hit, axis=1, keepdims=True)
        vc[at, :] = vr[:, at].T

    for h in halos:
        h.wait_recv()

    entry = iota((FULL, 1), 0)
    div, mod = orbital_of(entry)
    first = bits(iota((16, LANE), 1) == 0)
    count_all = nt(first, tab[:, FEAT:FEAT + LANE]).astype(BF16)
    count_own = nt(first, tab[RIM:RIM + A, FEAT:FEAT + LANE]).astype(BF16)
    lanes_own = iota((TILE, A), 1).astype(F32)
    lanes_near = iota((TILE, 2 * W), 1).astype(F32)

    def hits_row(at):
        own = bits(iota((A, TILE), 0).astype(F32) == vr[0:1, at])
        near = bits(iota((2 * W, TILE), 0).astype(F32) == vr[1:2, at])
        return own, near

    @pl.loop(0, ntile)
    def _(t):
        at = rows_at(t)
        own_hit, near_hit = hits_row(at)
        no = nn(count_own, own_hit)[0:1, :]
        near = nn(count_all, near_hit)[0:1, :]
        keep = (div < no) & (mod < near)
        mask_s[:, at] = bits(keep)
        xo = nn(bits(lanes_own == vc[at, 0:1]), tab[RIM:RIM + A, 0:FEAT])
        xn = nn(bits(lanes_near == vc[at, 1:2]), tab[:, 0:FEAT])
        xo_s[at, :] = xo.astype(BF16)
        xn_s[at, :] = xn.astype(BF16)
        prod = (xo * xn).astype(BF16)
        prod_s[at, :] = prod
        pre = nn(prod, wp_ref[...]) + nn(edge_ref[at, :], we_ref[...])
        sg = jax.nn.sigmoid(pre)
        act = (pre * sg).astype(BF16)
        act_s[at, :] = act
        ds_s[at, :] = sg * (1.0 + pre * (1.0 - sg))
        blk[:, at] = jnp.where(keep, nt(wbp[...], act), 0.0).astype(BF16)

    STEP = 2 * TILE

    def pack_blocks(d, dst):
        acc = jnp.zeros((FULL, C), F32)
        base = (d * C).astype(F32)
        slot_of = iota((STEP, C), 1).astype(F32)
        for j in range(T // STEP):
            at = slice(j * STEP, (j + 1) * STEP)
            acc = acc + nn(blk[:, at], bits(slot_of == vc[at, 2:3] - base))
        dst[d] = acc.astype(BF16)

    @pl.loop(1, D)
    def _(k):
        d = peer(k)
        pack_blocks(d, bs)
        exchange(bs, br, blk_s, blk_r, d, me).start()

    pack_blocks(me, br)

    dc[...] = jnp.zeros_like(dc)

    def collect(d):
        base = (d * C).astype(F32)
        slot_of = iota((C, STEP), 0).astype(F32)
        for j in range(T // STEP):
            at = slice(j * STEP, (j + 1) * STEP)
            dc[:, at] += nn(cr[d], bits(slot_of == vr[2:3, at] - base))

    collect(me)

    @pl.loop(1, D)
    def _(k):
        d = source(k)
        exchange(cs, cr, cot_s, cot_r, d, d).wait_recv()
        collect(d)

    gt[...] = jnp.zeros_like(gt)
    gp_ref[...] = jnp.zeros_like(gp_ref)
    ge_ref[...] = jnp.zeros_like(ge_ref)
    gba[...] = jnp.zeros_like(gba)

    @pl.loop(0, ntile)
    def _(t):
        at = rows_at(t)
        dblock = (dc[:, at] * mask_s[:, at].astype(F32)).astype(BF16)
        dact = tn(dblock, wbp[...])
        dpre = (dact * ds_s[at, :]).astype(BF16)
        gp_ref[...] += tn(prod_s[at, :], dpre)
        ge_ref[...] += tn(edge_ref[at, :], dpre)
        gba[...] += nn(dblock, act_s[at, :])
        dprod = nt(dpre, wp_ref[...])
        to_own = (dprod * xn_s[at, :].astype(F32)).astype(BF16)
        to_near = (dprod * xo_s[at, :].astype(F32)).astype(BF16)
        own_hit, near_hit = hits_row(at)
        gt[...] += nn(near_hit, to_near)
        gt[RIM:RIM + A, :] += nn(own_hit, to_own)

    if 2 * R > 4 * (FEAT + EDGE + FULL):
        g32[4 * (FEAT + EDGE + FULL):2 * R, :] = jnp.zeros((2 * R - 4 * (FEAT + EDGE + FULL), LANE), F32)
    for c in range(4):
        g32[c * FEAT:(c + 1) * FEAT, :] = gp_ref[:, c * LANE:(c + 1) * LANE]
        g32[4 * FEAT + c * EDGE:4 * FEAT + (c + 1) * EDGE, :] = ge_ref[:, c * LANE:(c + 1) * LANE]
    low = 4 * FEAT + 4 * EDGE
    for c in range(4):
        g32[low + c * FULL:low + (c + 1) * FULL, :] = gba[:, c * LANE:(c + 1) * LANE]
    gas[...] = g32[pl.ds(pl.multiple_of(other * R, 16), R), :].astype(BF16)
    swap = rcopy(gas, gar, sum_s, sum_r, me, other)
    swap.start()

    gtb[...] = gt[...].astype(BF16)
    grads = [
        rcopy(gtb.at[0:RIM], gr.at[0], grad_s.at[0], grad_r.at[0], prv, slab),
        rcopy(gtb.at[RIM + A:W], gr.at[1], grad_s.at[1], grad_r.at[1], nxt, slab),
        rcopy(gtb.at[W:W + RIM], gr.at[2], grad_s.at[2], grad_r.at[2], prv, other),
        rcopy(gtb.at[W + RIM + A:2 * W], gr.at[3], grad_s.at[3], grad_r.at[3], nxt, other),
        rcopy(gtb.at[W + RIM:W + RIM + A], grp, grad_s.at[4], grad_r.at[4], me, other),
    ]
    for g in grads:
        g.start()

    swap.wait_recv()
    hs[...] = (g32[pl.ds(pl.multiple_of(slab * R, 16), R), :] + gar[...].astype(F32)).astype(BF16)

    def piece(d, of=0):
        return pl.ds(pl.multiple_of(of * R + d * PIECE, 16), PIECE)

    def reduce_copy(d, at):
        return rcopy(hs.at[piece(d)], rb.at[at], red_s.at[d], red_r.at[at], d, slab)

    @pl.loop(1, D)
    def _(k):
        reduce_copy(peer(k), me).start()

    for g in grads:
        g.wait_recv()
    ag_ref[...] = gt[RIM:RIM + A, :] + grp[...].astype(F32)
    ag_ref[A - RIM:A, :] += gr[0].astype(F32) + gr[2].astype(F32)
    ag_ref[0:RIM, :] += gr[1].astype(F32) + gr[3].astype(F32)

    def add_up(k, total):
        s = source(k)
        reduce_copy(s, s).wait_recv()
        return total + rb[s].astype(F32)

    total = lax.fori_loop(1, D, add_up, g32[piece(me, slab), :] + gar[piece(me), :].astype(F32))
    fin[piece(me, slab), :] = total.astype(BF16)

    def gather_copy(d, at):
        return rcopy(fin.at[piece(at, slab)], fin.at[piece(at, slab)], all_s.at[d], all_r.at[at], d, slab)

    def forward_copy(s, of):
        return rcopy(fin.at[piece(s, of)], fin.at[piece(s, of)], fwd_s.at[s], fwd_r.at[s], me, other)

    @pl.loop(1, D)
    def _(k):
        gather_copy(peer(k), me).start()

    forward_copy(me, slab).start()

    def unpack(d):
        at = pl.ds(pl.multiple_of(d * C, C), C)
        bo_ref[0:CUT, at] = br[d, 0:CUT, :]
        bo_ref[CUT:BLOCK, at] = br[d, CUT:BLOCK, :]

    unpack(me)

    @pl.loop(1, D)
    def _(k):
        d = source(k)
        exchange(bs, br, blk_s, blk_r, d, d).wait_recv()
        unpack(d)

    @pl.loop(1, D)
    def _(k):
        s = source(k)
        gather_copy(s, s).wait_recv()
        forward_copy(s, slab).start()

    @pl.loop(0, D)
    def _(s):
        forward_copy(s, other).wait_recv()

    for c in range(4):
        gp_ref[:, c * LANE:(c + 1) * LANE] = fin[c * FEAT:(c + 1) * FEAT, :].astype(F32) * scale
        ge_ref[:, c * LANE:(c + 1) * LANE] = fin[4 * FEAT + c * EDGE:4 * FEAT + (c + 1) * EDGE, :].astype(F32) * scale
    for c in range(4):
        gb_ref[:, c * LANE:(c + 1) * LANE] = fin[low + c * FULL:low + c * FULL + BLOCK, :].astype(F32) * scale

    for h in halos + grads + [swap]:
        h.wait_send()

    @pl.loop(1, D)
    def _(k):
        d = peer(k)
        exchange(cs, cr, cot_s, cot_r, d, me).wait_send()
        exchange(bs, br, blk_s, blk_r, d, me).wait_send()
        reduce_copy(d, me).wait_send()
        gather_copy(d, me).wait_send()

    @pl.loop(0, D)
    def _(s):
        forward_copy(s, slab).wait_send()


def shards(features, orbitals, pair_list, owners, edge_feats, cotangent, w_pair, w_edge, w_block):
    A, FEAT = features.shape[1:]
    T = pair_list.shape[1]
    D = lax.axis_size("dom")
    S, BLOCK = cotangent.shape[1:]
    EDGE = edge_feats.shape[2]
    C = S // D
    CP = -(-C // LANE) * LANE
    W = A + 2 * RIM
    FULL = -(-BLOCK // 16) * 16
    flat = 4 * (FEAT + EDGE + FULL)
    PIECE = -(-flat // (2 * D * 16)) * 16
    R = D * PIECE
    scale = float(lax.axis_size("slab") * D * T) ** (-0.5)
    cot = cotangent[0].T
    if CP != C:
        cot = jnp.pad(cot.reshape(BLOCK, D, C), ((0, 0), (0, 0), (0, CP - C))).reshape(BLOCK, D * CP)
    dma = pltpu.SemaphoreType.DMA
    vmem = pl.BlockSpec(memory_space=pltpu.VMEM)
    outs = pl.pallas_call(
        functools.partial(kernel, D, CP, T, A, FEAT, EDGE, BLOCK, PIECE, scale),
        out_shape=(
            jax.ShapeDtypeStruct((BLOCK, D * CP), BF16),
            jax.ShapeDtypeStruct((A, FEAT), F32),
            jax.ShapeDtypeStruct((FEAT, FEAT), F32),
            jax.ShapeDtypeStruct((EDGE, FEAT), F32),
            jax.ShapeDtypeStruct((BLOCK, FEAT), F32),
        ),
        in_specs=[vmem] * 9,
        out_specs=(vmem,) * 5,
        scratch_shapes=[
            pltpu.VMEM((2 * W, FEAT + LANE), BF16),
            pltpu.VMEM((FULL, FEAT), BF16),
            pltpu.VMEM((D, FULL, CP), BF16),
            pltpu.VMEM((D, FULL, CP), BF16),
            pltpu.VMEM((D, FULL, CP), BF16),
            pltpu.VMEM((D, FULL, CP), BF16),
            pltpu.VMEM((8, T), F32),
            pltpu.VMEM((T, 8), F32),
            pltpu.VMEM((T, FEAT), BF16),
            pltpu.VMEM((T, FEAT), BF16),
            pltpu.VMEM((T, FEAT), BF16),
            pltpu.VMEM((T, FEAT), BF16),
            pltpu.VMEM((T, FEAT), F32),
            pltpu.VMEM((FULL, T), BF16),
            pltpu.VMEM((FULL, T), BF16),
            pltpu.VMEM((FULL, T), F32),
            pltpu.VMEM((2 * W, FEAT), F32),
            pltpu.VMEM((2 * W, FEAT), BF16),
            pltpu.VMEM((4, RIM, FEAT), BF16),
            pltpu.VMEM((A, FEAT), BF16),
            pltpu.VMEM((FULL, FEAT), F32),
            pltpu.VMEM((2 * R, LANE), F32),
            pltpu.VMEM((R, LANE), BF16),
            pltpu.VMEM((R, LANE), BF16),
            pltpu.VMEM((R, LANE), BF16),
            pltpu.VMEM((D, PIECE, LANE), BF16),
            pltpu.VMEM((2 * R, LANE), BF16),
            dma((5,)), dma((5,)), dma((D,)), dma((D,)), dma((D,)), dma((D,)), dma((5,)), dma((5,)),
            dma, dma, dma((D,)), dma((D,)), dma((D,)), dma((D,)), dma((D,)), dma((D,)),
        ],
        compiler_params=pltpu.CompilerParams(
            collective_id=0, has_side_effects=True, vmem_limit_bytes=56 * 1024 * 1024
        ),
        cost_estimate=pl.CostEstimate(flops=15 * 10**9, bytes_accessed=10**7, transcendentals=T * FEAT),
    )(features[0], orbitals, pair_list[0].T, owners[0].T, edge_feats[0], cot, w_pair, w_edge, w_block.T)
    blocks = outs[0]
    if CP != C:
        blocks = blocks.reshape(BLOCK, D, CP)[:, :, 0:C].reshape(BLOCK, S)
    return (blocks.T[None], outs[1][None], outs[2], outs[3], outs[4].T)


def solution(mesh):
    spread = P("slab", ("groups", "dom"), None)
    in_specs = (spread, P("slab", ("groups", "dom")), spread, spread, spread, spread, P(), P(), P())
    out_specs = (spread, spread, P("groups", None), P("groups", None), P("groups", None))
    return jax.shard_map(shards, mesh=mesh, in_specs=in_specs, out_specs=out_specs, check_vma=False)
```

time: 96.3 us -> 86.7 us (0.900)
  the two profiles are of different devices: /device:TPU:25 before, /device:TPU:1 now
where the time goes in v2:
time: 86.7 us; the launch traced here: 86.5 us
  Pallas kernels  80.2 us (93%)
  local copies, waits for them, and re-layouts  5.63 us (6%)
    pallas_call x1, Pallas kernels, shards(): pl.pallas_call(functools.partial(kernel, D, CP, T, A, FEAT, EDGE, BLOCK,...  80.2 us
    unnamed x13, local copies, waits for them, and re-layouts  5.63 us

profile of v2, /device:TPU:1, one launch (start us, length us, event | category | flops | bytes accessed | tf_op | source)
XLA Modules:
  0.0 86.5 jit_solution(14673325548957767193)
XLA Ops:
  0.6 80.2 %shard_map.128 = (bf16[169,3072]{1,0:T(8,128)(2,1)}, f32[128,512]{1,0:T(8,128)}, f32[512,512]{1,0:T(8,128)}, f32[128,512]{1,0:T(8,128)}, f32[169,512]{1,0:T(8,128)}) custom-call(bf16[128,512]{1,0:T(8,128)(2,1)} %bitcast.21, s32[1,128]{1,0:T(1,128)} %orb_ref.1, s32[2,2048]{1,0:T(2,128)} %bitcast.22, s32[1,2048]{1,0:T(1,128)} %bitcast.23, ...), custom_call_target="tpu_custom_call" | custom-call | flops 15000000512 | bytes 10000000 | tf_op jit(solution)/shard_map/pallas_call | solution.py:370
  80.8 0.0 copy-start.3
  80.8 0.0 copy-start
  80.8 2.4 %copy.19 = bf16[1,3072,169]{1,2,0:T(8,128)(2,1)} copy(bf16[1,3072,169]{1,2,0:T(8,128)(2,1)} %bitcast.15) | data formatting | bytes 2076672
  83.2 0.0 copy-done.3
  83.2 0.7 copy.20
  83.9 0.0 copy-done
  83.9 0.0 copy-start.2
  83.9 0.0 copy-start.1
  83.9 1.0 %copy.21 = f32[512,512]{1,0:T(8,128)} copy(f32[512,512]{1,0:T(8,128)S(1)} %copy-done) | data formatting | bytes 2097152
  84.9 0.1 copy-done.2
  85.0 0.7 copy.22
  85.7 0.0 copy-done.1
  85.7 0.7 copy.23
Async XLA Ops:
  80.8 2.4 %copy-start.3 = (f32[128,512]{1,0:T(8,128)S(1)}, f32[128,512]{1,0:T(8,128)}, u32[]{:S(2)}) copy-start(f32[128,512]{1,0:T(8,128)} %get-tuple-element.11) | copy-start | bytes 786436
  80.8 3.1 %copy-start = (f32[512,512]{1,0:T(8,128)S(1)}, f32[512,512]{1,0:T(8,128)}, u32[]{:S(2)}) copy-start(f32[512,512]{1,0:T(8,128)} %get-tuple-element.22) | copy-start | bytes 3145732
  83.9 1.1 %copy-start.2 = (f32[128,512]{1,0:T(8,128)S(1)}, f32[128,512]{1,0:T(8,128)}, u32[]{:S(2)}) copy-start(f32[128,512]{1,0:T(8,128)} %get-tuple-element.23) | copy-start | bytes 786436
  83.9 1.8 %copy-start.1 = (f32[169,512]{1,0:T(8,128)S(1)}, f32[169,512]{1,0:T(8,128)}, u32[]{:S(2)}) copy-start(f32[169,512]{1,0:T(8,128)} %get-tuple-element.14) | copy-start | bytes 1038340

commit v3 on v2

--- a/solution.py
+++ b/solution.py
@@ -44,10 +44,11 @@
 
 def kernel(
     D, C, T, A, FEAT, EDGE, BLOCK, PIECE, scale,
-    feat_ref, orb_ref, pair_ref, own_ref, edge_ref, cot_ref, wp_ref, we_ref, wb_ref,
+    feat_ref, orb_ref, pair_ref, own_ref, edge_in, cot_in, wp_in, we_ref, wb_ref,
     bo_ref, ag_ref, gp_ref, ge_ref, gb_ref,
     tab, wbp, cs, cr, bs, br, vr, vc, xo_s, xn_s, prod_s, act_s, ds_s, mask_s, blk, dc,
     gt, gtb, gr, grp, gba, g32, gas, gar, hs, rb, fin,
+    cot_ref, edge_ref, wp_ref, load_s,
     halo_s, halo_r, cot_s, cot_r, blk_s, blk_r, grad_s, grad_r, sum_s, sum_r, red_s, red_r,
     all_s, all_r, fwd_s, fwd_r,
 ):
@@ -79,6 +80,14 @@
     def rows_at(t):
         return pl.ds(pl.multiple_of(t * TILE, TILE), TILE)
 
+    loads = [
+        pltpu.make_async_copy(cot_in, cot_ref, load_s.at[0]),
+        pltpu.make_async_copy(edge_in, edge_ref, load_s.at[1]),
+        pltpu.make_async_copy(wp_in, wp_ref, load_s.at[2]),
+    ]
+    for load in loads:
+        load.start()
+
     barrier = pltpu.get_barrier_semaphore()
 
     @pl.loop(1, D)
@@ -91,6 +100,21 @@
     diag = jnp.where(iota((A, A), 0) == iota((A, A), 1), orb_ref[...].astype(F32), 0.0).astype(BF16)
     tab[RIM:RIM + A, 0:FEAT] = feat_ref[...]
     tab[RIM:RIM + A, FEAT:FEAT + LANE] = nn(diag, jnp.ones((A, LANE), BF16)).astype(BF16)
+    cs[:, CUT:FULL, :] = jnp.zeros((D, 16, C), BF16)
+    cr[me, CUT:FULL, :] = jnp.zeros((16, C), BF16)
+
+    def take_cot(d, dst):
+        at = pl.ds(pl.multiple_of(d * C, C), C)
+        dst[d, 0:CUT, :] = cot_ref[0:CUT, at]
+        dst[d, CUT:BLOCK, :] = cot_ref[CUT:BLOCK, at]
+
+    loads[0].wait()
+
+    @pl.loop(1, D)
+    def _(k):
+        take_cot(peer(k), cs)
+
+    take_cot(me, cr)
     pl.semaphore_wait(barrier, D + 2)
 
     head = tab.at[RIM:2 * RIM]
@@ -105,24 +129,12 @@
     for h in halos:
         h.start()
 
-    cs[:, CUT:FULL, :] = jnp.zeros((D, 16, C), BF16)
-    cr[me, CUT:FULL, :] = jnp.zeros((16, C), BF16)
-
-    def take_cot(d, dst):
-        at = pl.ds(pl.multiple_of(d * C, C), C)
-        dst[d, 0:CUT, :] = cot_ref[0:CUT, at]
-        dst[d, CUT:BLOCK, :] = cot_ref[CUT:BLOCK, at]
-
     def exchange(src, dst, ssem, rsem, d, at):
         return rcopy(src.at[d], dst.at[at], ssem.at[d], rsem.at[at], d, slab)
 
     @pl.loop(1, D)
     def _(k):
-        d = peer(k)
-        take_cot(d, cs)
-        exchange(cs, cr, cot_s, cot_r, d, me).start()
-
-    take_cot(me, cr)
+        exchange(cs, cr, cot_s, cot_r, peer(k), me).start()
 
     wbp[CUT:FULL, :] = jnp.zeros((16, FEAT), BF16)
     wbp[0:CUT, :] = wb_ref[0:CUT, :]
@@ -149,6 +161,8 @@
 
     for h in halos:
         h.wait_recv()
+    loads[1].wait()
+    loads[2].wait()
 
     entry = iota((FULL, 1), 0)
     div, mod = orbital_of(entry)
@@ -376,7 +390,7 @@
             jax.ShapeDtypeStruct((EDGE, FEAT), F32),
             jax.ShapeDtypeStruct((BLOCK, FEAT), F32),
         ),
-        in_specs=[vmem] * 9,
+        in_specs=[vmem] * 4 + [pl.BlockSpec(memory_space=pl.ANY)] * 3 + [vmem] * 2,
         out_specs=(vmem,) * 5,
         scratch_shapes=[
             pltpu.VMEM((2 * W, FEAT + LANE), BF16),
@@ -406,6 +420,10 @@
             pltpu.VMEM((R, LANE), BF16),
             pltpu.VMEM((D, PIECE, LANE), BF16),
             pltpu.VMEM((2 * R, LANE), BF16),
+            pltpu.VMEM((BLOCK, D * CP), BF16),
+            pltpu.VMEM((T, EDGE), BF16),
+            pltpu.VMEM((FEAT, FEAT), BF16),
+            dma((3,)),
             dma((5,)), dma((5,)), dma((D,)), dma((D,)), dma((D,)), dma((D,)), dma((5,)), dma((5,)),
             dma, dma, dma((D,)), dma((D,)), dma((D,)), dma((D,)), dma((D,)), dma((D,)),
         ],

time: 86.7 us -> 86.3 us (level)
  no operation moved by 1% of the time
where the time goes in v3:
time: 86.3 us; the launch traced here: 86.1 us
  Pallas kernels  79.8 us (92%)
  local copies, waits for them, and re-layouts  5.63 us (7%)
    pallas_call x1, Pallas kernels, shards(): pl.pallas_call(functools.partial(kernel, D, CP, T, A, FEAT, EDGE, BLOCK,...  79.8 us
    unnamed x13, local copies, waits for them, and re-layouts  5.63 us

profile of v3, /device:TPU:1, one launch (start us, length us, event | category | flops | bytes accessed | tf_op | source)
XLA Modules:
  0.0 86.1 jit_solution(8245547492640915267)
XLA Ops:
  0.6 79.8 %shard_map.128 = (bf16[169,3072]{1,0:T(8,128)(2,1)}, f32[128,512]{1,0:T(8,128)}, f32[512,512]{1,0:T(8,128)}, f32[128,512]{1,0:T(8,128)}, f32[169,512]{1,0:T(8,128)}) custom-call(bf16[128,512]{1,0:T(8,128)(2,1)} %bitcast.21, s32[1,128]{1,0:T(1,128)} %orb_ref.1, s32[2,2048]{1,0:T(2,128)} %bitcast.22, s32[1,2048]{1,0:T(1,128)} %bitcast.23, ...), custom_call_target="tpu_custom_call" | custom-call | flops 15000000512 | bytes 10000000 | tf_op jit(solution)/shard_map/pallas_call | solution.py:384
  80.4 0.0 copy-start.3
  80.4 0.0 copy-start
  80.4 2.4 %copy.19 = bf16[1,3072,169]{1,2,0:T(8,128)(2,1)} copy(bf16[1,3072,169]{1,2,0:T(8,128)(2,1)} %bitcast.15) | data formatting | bytes 2076672
  82.8 0.0 copy-done.3
  82.8 0.7 copy.20
  83.5 0.0 copy-done
  83.5 0.0 copy-start.2
  83.5 0.0 copy-start.1
  83.5 1.0 %copy.21 = f32[512,512]{1,0:T(8,128)} copy(f32[512,512]{1,0:T(8,128)S(1)} %copy-done) | data formatting | bytes 2097152
  84.5 0.1 copy-done.2
  84.6 0.7 copy.22
  85.3 0.0 copy-done.1
  85.3 0.7 copy.23
Async XLA Ops:
  80.4 2.4 %copy-start.3 = (f32[128,512]{1,0:T(8,128)S(1)}, f32[128,512]{1,0:T(8,128)}, u32[]{:S(2)}) copy-start(f32[128,512]{1,0:T(8,128)} %get-tuple-element.11) | copy-start | bytes 786436
  80.4 3.1 %copy-start = (f32[512,512]{1,0:T(8,128)S(1)}, f32[512,512]{1,0:T(8,128)}, u32[]{:S(2)}) copy-start(f32[512,512]{1,0:T(8,128)} %get-tuple-element.22) | copy-start | bytes 3145732
  83.5 1.1 %copy-start.2 = (f32[128,512]{1,0:T(8,128)S(1)}, f32[128,512]{1,0:T(8,128)}, u32[]{:S(2)}) copy-start(f32[128,512]{1,0:T(8,128)} %get-tuple-element.23) | copy-start | bytes 786436
  83.5 1.8 %copy-start.1 = (f32[169,512]{1,0:T(8,128)S(1)}, f32[169,512]{1,0:T(8,128)}, u32[]{:S(2)}) copy-start(f32[169,512]{1,0:T(8,128)} %get-tuple-element.14) | copy-start | bytes 1038340
